TPU v7x, 32 devices: a whole 2x2x4 slice. The times are simulated.
32 devices in a mesh: groups: 2 (over x), path: 8 (over z, y), cons: 2 (over core).
Axes of the slice: x: 2, y: 2, z: 4, core: 2. Of those that a mesh axis runs over, the one named last changes fastest.
Arguments:
- tile_values: bfloat16 [16, 2, 32, 128, 128], P(('groups', 'path'), 'cons'), parts along dimension 0, may hold values from -0.125 to 0.125
- row_blocks: int32 [16, 2, 32], P(('groups', 'path'), 'cons'), parts along dimension 0, may hold values from 0 to 15, as said below
- col_blocks: int32 [16, 2, 32], P(('groups', 'path'), 'cons'), parts along dimension 0, may hold values from 0 to 7
- path_cost: float32 [16384], P(('groups', 'path', 'cons')), parts along dimension 0, may hold values from -6 to 6
- path_bound: float32 [16384], P(('groups', 'path', 'cons')), parts along dimension 0, may hold values from 0.5 to 2
- primal_start: float32 [16384], P(('groups', 'path', 'cons')), parts along dimension 0, may hold values from 0 to 1
- dual_start: float32 [8192], P(('groups', 'path', 'cons')), parts along dimension 0, may hold values from 0 to 1
- row_limits: float32 [8192], P(('groups', 'path', 'cons')), parts along dimension 0, may hold values from -6 to 6
- step_size: float32 [2], P('groups'), parts along dimension 0, may hold values from 0.3 to 0.45
- weight_start: float32 [2], P('groups'), parts along dimension 0, may hold values from 0.5 to 2
- restart_flags: int32 [12], P('groups'), parts along dimension 0, may hold values from 0 to 1
Outputs:
- primal_out: float32 [16384], P(('groups', 'path', 'cons')), parts along dimension 0
- dual_out: float32 [8192], P(('groups', 'path', 'cons')), parts along dimension 0
- link_loads: float32 [8192], P(('groups', 'path', 'cons')), parts along dimension 0
There are 2 independent parts, one for each index of `groups`. A program takes and returns all parts, laid end to end along the dimension named above; each array names one. Nothing has to cross between parts.
Inputs may be any that keep to these rules, and one draw needn't show every extreme that they name: `row_blocks`: row block of a tile inside its constraint half; for every device and every index o of path, at most 8 of the device's tiles lie in row blocks 2 * o to 2 * o + 1, and on every device some index o has exactly 8.
All inputs are finite; a program needn't handle non-finite values.
Results may differ from a plain program's by a relative error of at most 0.0031.
Values may be sent and summed in bfloat16 or wider, within the bound.
A program may use at most 64 MiB of HBM per device.

v0:
```python
import jax
import jax.numpy as jnp
from jax import lax
from jax.sharding import PartitionSpec as P


def tile_rows(tile_values, col_blocks, primal_low):
    blocks = primal_low.reshape(-1, tile_values.shape[-1])
    picked = blocks[col_blocks]
    return jnp.einsum("tij,tj->ti", tile_values, picked, preferred_element_type=jnp.float32)


def col_partial(tile_values, picked, col_blocks, col_count):
    products = jnp.einsum("tij,ti->tj", tile_values, picked, preferred_element_type=jnp.float32)
    return jax.ops.segment_sum(products, col_blocks, num_segments=col_count).reshape(-1)


def shards(
    tile_values,
    row_blocks,
    col_blocks,
    path_cost,
    path_bound,
    primal_start,
    dual_start,
    row_limits,
    step_size,
    weight_start,
    restart_flags,
):
    epsilon = 1e-06
    tile_values = tile_values[0, 0]
    row_blocks = row_blocks[0, 0]
    col_blocks = col_blocks[0, 0]
    edge = tile_values.shape[-1]
    primal_width = path_cost.shape[0]
    dual_width = row_limits.shape[0]
    col_count = primal_width * lax.axis_size("cons") // edge
    own_blocks = dual_width // edge
    path_count = lax.axis_size("path")
    tile_count = row_blocks.shape[0]
    capacity = max(2, (2 * tile_count + path_count - 1) // path_count)
    primal_now = primal_start
    dual_now = dual_start
    owners = row_blocks // own_blocks
    positions = jnp.arange(tile_count, dtype=jnp.int32)
    earlier = (owners[:, None] == owners[None, :]) & (positions[None, :] < positions[:, None])
    ranks = jnp.sum(earlier.astype(jnp.int32), axis=1)
    targets = owners * capacity + ranks
    slot_rows = (
        jnp.full((path_count * capacity,), -1, jnp.int32).at[targets].set(row_blocks % own_blocks)
    )
    arrived = lax.all_to_all(slot_rows, "path", split_axis=0, concat_axis=0, tiled=True)
    selector = (arrived[None, :] == jnp.arange(own_blocks, dtype=jnp.int32)[:, None]).astype(
        jnp.float32
    )
    reply_rows = jnp.maximum(arrived, 0)

    def primal_product(primal_low):
        primal_low = lax.all_gather(primal_low, "cons", axis=0, tiled=True)
        products = tile_rows(tile_values, col_blocks, primal_low)
        outgoing = jnp.zeros((path_count * capacity, edge), jnp.float32).at[targets].set(products)
        incoming = lax.all_to_all(outgoing, "path", split_axis=0, concat_axis=0, tiled=True)
        return jnp.dot(selector, incoming, precision=lax.Precision.HIGHEST).reshape(-1)

    anchor_primal = primal_now
    anchor_dual = dual_now
    primal_sum = jnp.zeros_like(primal_now)
    dual_sum = jnp.zeros_like(dual_now)
    steps_taken = jnp.zeros((), jnp.float32)
    eta = step_size[0]
    weight = weight_start[0]
    for turn_index in range(restart_flags.shape[0]):
        dual_low = dual_now.astype(jnp.bfloat16)
        replies = dual_low.reshape(own_blocks, edge)[reply_rows]
        returned = lax.all_to_all(replies, "path", split_axis=0, concat_axis=0, tiled=True)
        picked = returned[targets]
        partial_terms = col_partial(tile_values, picked, col_blocks, col_count)
        gradient = lax.psum_scatter(partial_terms, "cons", scatter_dimension=0, tiled=True)
        primal_next = jnp.clip(primal_now - eta / weight * (path_cost + gradient), 0.0, path_bound)
        extrapolated = (2.0 * primal_next - primal_now).astype(jnp.bfloat16)
        activity = primal_product(extrapolated)
        dual_next = jnp.maximum(dual_now + eta * weight * (activity - row_limits), 0.0)
        primal_sum = primal_sum + primal_next
        dual_sum = dual_sum + dual_next
        steps_taken = steps_taken + 1.0
        primal_mean = primal_sum / steps_taken
        dual_mean = dual_sum / steps_taken
        primal_shift = primal_mean - anchor_primal
        dual_shift = dual_mean - anchor_dual
        primal_move, dual_move = lax.psum(
            (jnp.sum(primal_shift * primal_shift), jnp.sum(dual_shift * dual_shift)),
            ("path", "cons"),
        )
        candidate = jnp.sqrt(
            weight * jnp.sqrt(dual_move + epsilon) / jnp.sqrt(primal_move + epsilon)
        )
        restart = restart_flags[turn_index] == 1
        primal_now = jnp.where(restart, primal_mean, primal_next)
        dual_now = jnp.where(restart, dual_mean, dual_next)
        anchor_primal = jnp.where(restart, primal_mean, anchor_primal)
        anchor_dual = jnp.where(restart, dual_mean, anchor_dual)
        primal_sum = jnp.where(restart, jnp.zeros_like(primal_sum), primal_sum)
        dual_sum = jnp.where(restart, jnp.zeros_like(dual_sum), dual_sum)
        steps_taken = jnp.where(restart, jnp.zeros((), jnp.float32), steps_taken)
        weight = jnp.where(restart, candidate, weight)
    loads = primal_product(primal_now.astype(jnp.bfloat16))
    return (primal_now, dual_now, loads)


def solution(mesh):
    in_specs = (
        P(("groups", "path"), "cons", None, None, None),
        P(("groups", "path"), "cons", None),
        P(("groups", "path"), "cons", None),
        P(("groups", "path", "cons")),
        P(("groups", "path", "cons")),
        P(("groups", "path", "cons")),
        P(("groups", "path", "cons")),
        P(("groups", "path", "cons")),
        P("groups"),
        P("groups"),
        P("groups"),
    )
    out_specs = (
        P(("groups", "path", "cons")),
        P(("groups", "path", "cons")),
        P(("groups", "path", "cons")),
    )
    return jax.shard_map(shards, mesh=mesh, in_specs=in_specs, out_specs=out_specs, check_vma=False)
```

profile of v0, /device:TPU:0, one launch (start us, length us, event | category | flops | bytes accessed | tf_op | source)
XLA Modules:
  0.0 356.9 jit_solution(11803322861526937581)
XLA Ops:
  3.4 7.4 %all-to-all-start = ((s32[8,8,1]{1,2,0:T(1,128)}), s32[8,8,1]{1,2,0:T(1,128)S(1)}, u32[]{:S(2)}, u32[]{:S(2)}) async-start(s32[8,8,1]{1,2,0:T(1,128)} %bitcast.14), calls=%async_computation | async-start | bytes 8192 | tf_op jit(solution)/shard_map/all_to_all | solution.py:53
  11.5 5.8 %all-to-all-done = s32[8,8,1]{1,2,0:T(1,128)S(1)} async-done(((s32[8,8,1]{1,2,0:T(1,128)}), s32[8,8,1]{1,2,0:T(1,128)S(1)}, u32[]{:S(2)}, u32[]{:S(2)}) %all-to-all-start) | async-done | bytes 288 | tf_op jit(solution)/shard_map/all_to_all | solution.py:53
  19.8 3.3 all-to-all-start.1
  38.8 3.3 all-to-all-start.2
  42.3 6.5 %all-to-all-done.2 = f32[8,8,128]{2,1,0:T(8,128)S(1)} async-done(((f32[8,8,128]{2,1,0:T(8,128)}), f32[8,8,128]{2,1,0:T(8,128)S(1)}, u32[]{:S(2)}, u32[]{:S(2)}) %all-to-all-start.2) | async-done | bytes 32800 | tf_op jit(solution)/shard_map/all_to_all | solution.py:63
  50.8 3.5 all-to-all-start.3
  55.5 33.1 %all-reduce.10 = (f32[]{:T(128)}, f32[]{:T(128)}) all-reduce(f32[]{:T(128)} %get-tuple-element.40, f32[]{:T(128)} %get-tuple-element.33), channel_id=1, replica_groups=mesh['groups'=2,'path'=8,'cons'=2] {'path','cons'}, use_global_device_ids=true, to_apply=%region_6.7 | all-reduce | flops 2 | bytes 16 | tf_op jit(solution)/shard_map/psum | solution.py:91
  99.2 3.3 all-to-all-start.4
  103.2 5.9 %all-to-all-done.4 = f32[8,8,128]{2,1,0:T(8,128)S(1)} async-done(((f32[8,8,128]{2,1,0:T(8,128)}), f32[8,8,128]{2,1,0:T(8,128)S(1)}, u32[]{:S(2)}, u32[]{:S(2)}) %all-to-all-start.4) | async-done | bytes 32800 | tf_op jit(solution)/shard_map/all_to_all | solution.py:63
  111.1 3.3 all-to-all-start.5
  114.5 33.1 %all-reduce.9 = (f32[]{:T(128)}, f32[]{:T(128)}) all-reduce(f32[]{:T(128)} %get-tuple-element.31, f32[]{:T(128)} %get-tuple-element.29), channel_id=1, replica_groups=mesh['groups'=2,'path'=8,'cons'=2] {'path','cons'}, use_global_device_ids=true, to_apply=%region_13.14 | all-reduce | flops 2 | bytes 16 | tf_op jit(solution)/shard_map/psum | solution.py:91
  158.2 3.3 all-to-all-start.6
  162.2 6.0 %all-to-all-done.6 = f32[8,8,128]{2,1,0:T(8,128)S(1)} async-done(((f32[8,8,128]{2,1,0:T(8,128)}), f32[8,8,128]{2,1,0:T(8,128)S(1)}, u32[]{:S(2)}, u32[]{:S(2)}) %all-to-all-start.6) | async-done | bytes 32800 | tf_op jit(solution)/shard_map/all_to_all | solution.py:63
  170.2 3.3 all-to-all-start.7
  173.5 33.1 %all-reduce.8 = (f32[]{:T(128)}, f32[]{:T(128)}) all-reduce(f32[]{:T(128)} %get-tuple-element.25, f32[]{:T(128)} %get-tuple-element.21), channel_id=1, replica_groups=mesh['groups'=2,'path'=8,'cons'=2] {'path','cons'}, use_global_device_ids=true, to_apply=%region_20.21 | all-reduce | flops 2 | bytes 16 | tf_op jit(solution)/shard_map/psum | solution.py:91
  217.2 3.3 all-to-all-start.8
  221.2 6.0 %all-to-all-done.8 = f32[8,8,128]{2,1,0:T(8,128)S(1)} async-done(((f32[8,8,128]{2,1,0:T(8,128)}), f32[8,8,128]{2,1,0:T(8,128)S(1)}, u32[]{:S(2)}, u32[]{:S(2)}) %all-to-all-start.8) | async-done | bytes 32800 | tf_op jit(solution)/shard_map/all_to_all | solution.py:63
  229.2 3.3 all-to-all-start.9
  232.5 33.1 %all-reduce.7 = (f32[]{:T(128)}, f32[]{:T(128)}) all-reduce(f32[]{:T(128)} %get-tuple-element.19, f32[]{:T(128)} %get-tuple-element.17), channel_id=1, replica_groups=mesh['groups'=2,'path'=8,'cons'=2] {'path','cons'}, use_global_device_ids=true, to_apply=%region_27.28 | all-reduce | flops 2 | bytes 16 | tf_op jit(solution)/shard_map/psum | solution.py:91
  276.3 3.3 all-to-all-start.10
  280.2 6.0 %all-to-all-done.10 = f32[8,8,128]{2,1,0:T(8,128)S(1)} async-done(((f32[8,8,128]{2,1,0:T(8,128)}), f32[8,8,128]{2,1,0:T(8,128)S(1)}, u32[]{:S(2)}, u32[]{:S(2)}) %all-to-all-start.10) | async-done | bytes 32800 | tf_op jit(solution)/shard_map/all_to_all | solution.py:63
  292.2 33.2 %all-reduce.6 = (f32[]{:T(128)}, f32[]{:T(128)}) all-reduce(f32[]{:T(128)} %get-tuple-element.38, f32[]{:T(128)} %get-tuple-element.36), channel_id=1, replica_groups=mesh['groups'=2,'path'=8,'cons'=2] {'path','cons'}, use_global_device_ids=true, to_apply=%region_34.35 | all-reduce | flops 2 | bytes 16 | tf_op jit(solution)/shard_map/psum | solution.py:91
  345.9 3.6 %all-to-all-start.12 = ((f32[8,8,128]{2,1,0:T(8,128)}), f32[8,8,128]{2,1,0:T(8,128)S(1)}, u32[]{:S(2)}, u32[]{:S(2)}) async-start(f32[8,8,128]{2,1,0:T(8,128)} %bitcast.92), calls=%async_computation.12 | async-start | bytes 65536 | tf_op jit(solution)/shard_map/all_to_all | solution.py:63
  350.2 6.0 %all-to-all-done.12 = f32[8,8,128]{2,1,0:T(8,128)S(1)} async-done(((f32[8,8,128]{2,1,0:T(8,128)}), f32[8,8,128]{2,1,0:T(8,128)S(1)}, u32[]{:S(2)}, u32[]{:S(2)}) %all-to-all-start.12) | async-done | bytes 32800 | tf_op jit(solution)/shard_map/all_to_all | solution.py:63
  (146 shorter events, 90.6 us)
Async XLA Ops:
  0.6 29.6 %copy-start = (bf16[1,1,32,128,128]{4,3,2,1,0:T(8,128)(2,1)S(1)}, bf16[1,1,32,128,128]{4,3,2,1,0:T(8,128)(2,1)}, u32[]{:S(2)}) copy-start(bf16[1,1,32,128,128]{4,3,2,1,0:T(8,128)(2,1)} %param.11) | copy-start | bytes 3145732
  1.4 0.7 copy-start.7
  3.4 7.4 %copy-start.6 = (f32[256]{0:T(256)S(1)}, f32[256]{0:T(256)}, u32[]{:S(2)}) copy-start(f32[256]{0:T(256)} %param.17) | copy-start | bytes 3076
  3.4 13.9 %all-to-all-start = ((s32[8,8,1]{1,2,0:T(1,128)}), s32[8,8,1]{1,2,0:T(1,128)S(1)}, u32[]{:S(2)}, u32[]{:S(2)}) async-start(s32[8,8,1]{1,2,0:T(1,128)} %bitcast.14), calls=%async_computation | async-start | bytes 8192 | tf_op jit(solution)/shard_map/all_to_all | solution.py:53
  10.8 0.7 copy-start.8
  19.8 9.9 %all-to-all-start.1 = ((bf16[8,8,128]{2,1,0:T(8,128)(2,1)}), bf16[8,8,128]{2,1,0:T(8,128)(2,1)S(1)}, u32[]{:S(2)}, u32[]{:S(2)}) async-start(bf16[8,8,128]{2,1,0:T(8,128)(2,1)} %bitcast.15), calls=%async_computation.1 | async-start | bytes 32768 | tf_op jit(solution)/shard_map/all_to_all | solution.py:76
  24.5 0.7 copy-start.9
  31.4 2.5 copy-start.1
  31.4 2.5 copy-start.2
  31.4 2.5 copy-start.3
  38.8 10.0 %all-to-all-start.2 = ((f32[8,8,128]{2,1,0:T(8,128)}), f32[8,8,128]{2,1,0:T(8,128)S(1)}, u32[]{:S(2)}, u32[]{:S(2)}) async-start(f32[8,8,128]{2,1,0:T(8,128)} %bitcast.27), calls=%async_computation.2 | async-start | bytes 65536 | tf_op jit(solution)/shard_map/all_to_all | solution.py:63
  42.2 6.6 %copy-start.4 = (f32[256]{0:T(256)S(1)}, f32[256]{0:T(256)}, u32[]{:S(2)}) copy-start(f32[256]{0:T(256)} %param.18) | copy-start | bytes 3076
  50.8 3.5 copy-start.5
  50.8 39.3 %all-to-all-start.3 = ((bf16[8,8,128]{2,1,0:T(8,128)(2,1)}), bf16[8,8,128]{2,1,0:T(8,128)(2,1)S(1)}, u32[]{:S(2)}, u32[]{:S(2)}) async-start(bf16[8,8,128]{2,1,0:T(8,128)(2,1)} %bitcast.31), calls=%async_computation.3 | async-start | bytes 32768 | tf_op jit(solution)/shard_map/all_to_all | solution.py:76
  99.2 10.0 %all-to-all-start.4 = ((f32[8,8,128]{2,1,0:T(8,128)}), f32[8,8,128]{2,1,0:T(8,128)S(1)}, u32[]{:S(2)}, u32[]{:S(2)}) async-start(f32[8,8,128]{2,1,0:T(8,128)} %bitcast.40), calls=%async_computation.4 | async-start | bytes 65536 | tf_op jit(solution)/shard_map/all_to_all | solution.py:63
  111.1 37.9 %all-to-all-start.5 = ((bf16[8,8,128]{2,1,0:T(8,128)(2,1)}), bf16[8,8,128]{2,1,0:T(8,128)(2,1)S(1)}, u32[]{:S(2)}, u32[]{:S(2)}) async-start(bf16[8,8,128]{2,1,0:T(8,128)(2,1)} %bitcast.44), calls=%async_computation.5 | async-start | bytes 32768 | tf_op jit(solution)/shard_map/all_to_all | solution.py:76
  158.2 10.0 %all-to-all-start.6 = ((f32[8,8,128]{2,1,0:T(8,128)}), f32[8,8,128]{2,1,0:T(8,128)S(1)}, u32[]{:S(2)}, u32[]{:S(2)}) async-start(f32[8,8,128]{2,1,0:T(8,128)} %bitcast.53), calls=%async_computation.6 | async-start | bytes 65536 | tf_op jit(solution)/shard_map/all_to_all | solution.py:63
  170.2 37.9 %all-to-all-start.7 = ((bf16[8,8,128]{2,1,0:T(8,128)(2,1)}), bf16[8,8,128]{2,1,0:T(8,128)(2,1)S(1)}, u32[]{:S(2)}, u32[]{:S(2)}) async-start(bf16[8,8,128]{2,1,0:T(8,128)(2,1)} %bitcast.57), calls=%async_computation.7 | async-start | bytes 32768 | tf_op jit(solution)/shard_map/all_to_all | solution.py:76
  217.2 10.0 %all-to-all-start.8 = ((f32[8,8,128]{2,1,0:T(8,128)}), f32[8,8,128]{2,1,0:T(8,128)S(1)}, u32[]{:S(2)}, u32[]{:S(2)}) async-start(f32[8,8,128]{2,1,0:T(8,128)} %bitcast.66), calls=%async_computation.8 | async-start | bytes 65536 | tf_op jit(solution)/shard_map/all_to_all | solution.py:63
  229.2 38.0 %all-to-all-start.9 = ((bf16[8,8,128]{2,1,0:T(8,128)(2,1)}), bf16[8,8,128]{2,1,0:T(8,128)(2,1)S(1)}, u32[]{:S(2)}, u32[]{:S(2)}) async-start(bf16[8,8,128]{2,1,0:T(8,128)(2,1)} %bitcast.70), calls=%async_computation.9 | async-start | bytes 32768 | tf_op jit(solution)/shard_map/all_to_all | solution.py:76
  276.3 10.0 %all-to-all-start.10 = ((f32[8,8,128]{2,1,0:T(8,128)}), f32[8,8,128]{2,1,0:T(8,128)S(1)}, u32[]{:S(2)}, u32[]{:S(2)}) async-start(f32[8,8,128]{2,1,0:T(8,128)} %bitcast.79), calls=%async_computation.10 | async-start | bytes 65536 | tf_op jit(solution)/shard_map/all_to_all | solution.py:63
  288.2 38.6 %all-to-all-start.11 = ((bf16[8,8,128]{2,1,0:T(8,128)(2,1)}), bf16[8,8,128]{2,1,0:T(8,128)(2,1)S(1)}, u32[]{:S(2)}, u32[]{:S(2)}) async-start(bf16[8,8,128]{2,1,0:T(8,128)(2,1)} %bitcast.83), calls=%async_computation.11 | async-start | bytes 32768 | tf_op jit(solution)/shard_map/all_to_all | solution.py:76
  336.0 10.0 %all-to-all-start.13 = ((f32[8,8,128]{2,1,0:T(8,128)}), f32[8,8,128]{2,1,0:T(8,128)S(1)}, u32[]{:S(2)}, u32[]{:S(2)}) async-start(f32[8,8,128]{2,1,0:T(8,128)} %bitcast.98), calls=%async_computation.13 | async-start | bytes 65536 | tf_op jit(solution)/shard_map/all_to_all | solution.py:63
  345.9 10.3 %all-to-all-start.12 = ((f32[8,8,128]{2,1,0:T(8,128)}), f32[8,8,128]{2,1,0:T(8,128)S(1)}, u32[]{:S(2)}, u32[]{:S(2)}) async-start(f32[8,8,128]{2,1,0:T(8,128)} %bitcast.92), calls=%async_computation.12 | async-start | bytes 65536 | tf_op jit(solution)/shard_map/all_to_all | solution.py:63
where the time goes:
time: 358 us; the launch traced here: 357 us
  blocking collectives  193 us (54%)
  starting transfers between devices  51.1 us (14%)
  waiting for transfers between devices  47.8 us (13%)
  local copies, waits for them, and re-layouts  29 us (8%)
  between operations  14 us (4%)
  other arithmetic  11.6 us (3%)
  matrix products  10.6 us (3%)
    psum x5, blocking collectives, shards(): lax.psum((jnp.sum(primal_shift * primal_shift), jnp.sum(dual_shift * dual...  166 us
    all_to_all x7, waiting for transfers between devices, primal_product(): lax.all_to_all(outgoing, 'path', split_axis=0, concat_axis=0, tiled=True)  38.7 us
    all_to_all x7, starting transfers between devices, primal_product(): lax.all_to_all(outgoing, 'path', split_axis=0, concat_axis=0, tiled=True)  23.6 us
    all_to_all x6, starting transfers between devices, shards(): lax.all_to_all(replies, 'path', split_axis=0, concat_axis=0, tiled=True)  20.1 us
    unnamed x6, blocking collectives  14.8 us
    all_gather x7, blocking collectives, primal_product(): primal_low = lax.all_gather(primal_low, 'cons', axis=0, tiled=True)  12.4 us
    scatter x7, local copies, waits for them, and re-layouts, primal_product(): jnp.zeros((path_count * capacity, edge), jnp.float32).at[targets]  8.69 us
    all_to_all x1, starting transfers between devices, shards(): lax.all_to_all(slot_rows, 'path', split_axis=0, concat_axis=0, tiled=True)  7.41 us
  transfers between devices with their start and end apart: 14, of which 9 were waited for; matrix products, arithmetic and copies ran while one was open for 1% of the time, Pallas kernels for 0%

commit v1 on v0

v1 whole, which is shorter than its diff:
```python
import functools
import jax
import jax.numpy as jnp
from jax import lax
from jax.experimental import pallas as pl
from jax.experimental.pallas import tpu as pltpu
from jax.sharding import PartitionSpec as P

LANES = 128
EPSILON = 1e-06


def kernel(
    n,
    iters,
    tiles_hbm,
    rows_s,
    cols_s,
    cost_in,
    bound_in,
    primal_in,
    dual_in,
    limits_in,
    step_s,
    weight_s,
    flags_s,
    primal_out,
    dual_out,
    loads_out,
    tiles,
    turned,
    start_buf,
    flows,
    dual_buf,
    grad_out,
    grad_in,
    act_out,
    act_in,
    tile_sem,
    start_send,
    start_recv,
    dual_send,
    dual_recv,
    grad_send,
    grad_recv,
    act_send,
    act_recv,
):
    me = lax.axis_index("path")
    core = lax.axis_index("cons")
    other = 1 - core
    count = tiles.shape[0]
    half = cost_in.shape[0]
    own = dual_in.shape[0]
    blocks = 2 * half
    unroll = n <= 8

    def peers(body):
        def step(k, carry):
            body(lax.rem(me + k, n))
            return carry

        lax.fori_loop(1, n, step, 0, unroll=unroll)

    tile_copy = pltpu.make_async_copy(tiles_hbm.at[0, 0], tiles, tile_sem)
    tile_copy.start()
    barrier = pltpu.get_barrier_semaphore()
    peers(lambda q: pl.semaphore_signal(barrier, inc=1, device_id={"path": q}))
    pl.semaphore_signal(barrier, inc=1, device_id={"cons": other})

    start_buf[core, 0] = cost_in[...]
    start_buf[core, 1] = bound_in[...]
    start_buf[core, 2] = primal_in[...]
    dual_buf[me, pl.ds(0, own)] = dual_in[...]
    dual_buf[me, pl.ds(own, 2)] = jnp.zeros((2, LANES), jnp.float32)
    pl.semaphore_wait(barrier, n)

    def dual_copy(source, q):
        return pltpu.make_async_remote_copy(
            src_ref=dual_buf.at[source],
            dst_ref=dual_buf.at[source],
            send_sem=dual_send.at[q],
            recv_sem=dual_recv.at[source],
            device_id={"path": q},
        )

    def act_copy(source, q, rows):
        return pltpu.make_async_remote_copy(
            src_ref=act_out.at[q, pl.ds(0, rows)],
            dst_ref=act_in.at[source, pl.ds(0, rows)],
            send_sem=act_send.at[q],
            recv_sem=act_recv.at[source],
            device_id={"path": q},
        )

    def grad_copy(slot):
        return pltpu.make_async_remote_copy(
            src_ref=grad_out.at[slot],
            dst_ref=grad_in.at[slot],
            send_sem=grad_send.at[slot],
            recv_sem=grad_recv.at[slot],
            device_id={"cons": other},
        )

    def start_copy(slot):
        return pltpu.make_async_remote_copy(
            src_ref=start_buf.at[slot],
            dst_ref=start_buf.at[slot],
            send_sem=start_send,
            recv_sem=start_recv,
            device_id={"cons": other},
        )

    peers(lambda q: dual_copy(me, q).start())
    start_copy(core).start()
    tile_copy.wait()
    for t in range(count):
        turned[t] = tiles[t].T
    start_copy(other).wait_recv()

    def whole(item):
        return jnp.concatenate([start_buf[0, item], start_buf[1, item]], axis=0)

    cost, bound, primal = whole(0), whole(1), whole(2)
    start_copy(core).wait_send()
    dual = dual_in[...]
    limits = limits_in[...]
    eta = step_s[0]
    weight = jnp.full((1, LANES), weight_s[0], jnp.float32)
    anchor_primal, anchor_dual = primal, dual
    primal_sum, dual_sum = jnp.zeros_like(primal), jnp.zeros_like(dual)
    taken = jnp.zeros((1, LANES), jnp.float32)
    col_iota = lax.broadcasted_iota(jnp.int32, (blocks, LANES), 0)

    for turn in range(iters):
        slot = turn % 2
        last = turn == iters - 1
        peers(lambda q: dual_copy(q, q).wait_recv())
        parts = []
        for t in range(count):
            row = rows_s[t]
            line = dual_buf[row // own, pl.ds(row % own, 1)]
            parts.append(jnp.where(col_iota == cols_s[t], line, 0.0).astype(jnp.bfloat16))
        left = jnp.concatenate(parts, axis=1)
        partial = jnp.dot(
            left, tiles[...].reshape(count * LANES, LANES), preferred_element_type=jnp.float32
        )
        if turn >= 2:
            grad_copy(slot).wait_send()
        grad_out[slot, pl.ds(0, blocks)] = partial
        moves = jnp.sum(dual_buf[:, own, :], axis=0, keepdims=True)
        grad_out[slot, pl.ds(blocks, 8)] = jnp.broadcast_to(moves, (8, LANES))
        grad_copy(slot).start()
        primal_moves = jnp.sum(dual_buf[:, own + 1, :], axis=0, keepdims=True)
        primal_move = jnp.sum(primal_moves, axis=1, keepdims=True)
        grad_copy(slot).wait_recv()
        gradient = partial + grad_in[slot, pl.ds(0, blocks)]
        if turn > 0:
            moves = moves + grad_in[slot, pl.ds(blocks, 1)]
            dual_move = jnp.sum(moves, axis=1, keepdims=True)
            candidate = jnp.sqrt(
                weight * jnp.sqrt(dual_move + EPSILON) / jnp.sqrt(primal_move + EPSILON)
            )
            weight = jnp.where(flags_s[turn - 1] == 1, candidate, weight)
        restart = flags_s[turn] == 1
        primal_next = jnp.clip(primal - eta / weight * (cost + gradient), 0.0, bound)
        extrapolated = 2.0 * primal_next - primal
        primal_sum = primal_sum + primal_next
        taken = taken + 1.0
        primal_mean = primal_sum / taken
        shift = primal_mean - anchor_primal
        primal_part = jnp.sum(shift * shift, axis=0, keepdims=True)
        primal = jnp.where(restart, primal_mean, primal_next)
        anchor_primal = jnp.where(restart, primal_mean, anchor_primal)
        primal_sum = jnp.where(restart, 0.0, primal_sum)

        rows = 2 * own if last else own
        row_iota = lax.broadcasted_iota(jnp.int32, (n * rows, LANES), 0)
        parts = []
        lines = [extrapolated, primal] if last else [extrapolated]
        if turn > 0:
            peers(lambda q: act_copy(me, q, own).wait_send())
        for index, line in enumerate(lines):
            flows[index] = line
        for t in range(count):
            row, col = rows_s[t], cols_s[t]
            spot = (row // own) * rows + row % own
            piece = jnp.zeros((n * rows, LANES), jnp.float32)
            for index in range(len(lines)):
                line = flows[index, pl.ds(col, 1)]
                piece = jnp.where(row_iota == spot + index * own, line, piece)
            parts.append(piece.astype(jnp.bfloat16))
        left = jnp.concatenate(parts, axis=1)
        activity = jnp.dot(
            left, turned[...].reshape(count * LANES, LANES), preferred_element_type=jnp.float32
        )
        for q in range(n):
            act_out[q, pl.ds(0, rows)] = activity[q * rows : (q + 1) * rows]
        peers(lambda q: act_copy(me, q, rows).start())
        act_in[me, pl.ds(0, rows)] = act_out[me, pl.ds(0, rows)]
        peers(lambda q: dual_copy(me, q).wait_send())
        peers(lambda q: act_copy(q, q, rows).wait_recv())
        total = jnp.sum(act_in[:, pl.ds(0, rows)], axis=0)
        dual_next = jnp.maximum(dual + eta * weight * (total[:own] - limits), 0.0)
        dual_sum = dual_sum + dual_next
        dual_mean = dual_sum / taken
        shift = dual_mean - anchor_dual
        dual = jnp.where(restart, dual_mean, dual_next)
        anchor_dual = jnp.where(restart, dual_mean, anchor_dual)
        dual_sum = jnp.where(restart, 0.0, dual_sum)
        taken = jnp.where(restart, 0.0, taken)
        if not last:
            dual_buf[me, pl.ds(0, own)] = dual
            dual_buf[me, pl.ds(own, 1)] = jnp.sum(shift * shift, axis=0, keepdims=True)
            dual_buf[me, pl.ds(own + 1, 1)] = primal_part
            peers(lambda q: dual_copy(me, q).start())

    primal_out[...] = jnp.where(core == 0, primal[:half], primal[half:])
    dual_out[...] = dual
    loads_out[...] = total[own:]
    peers(lambda q: act_copy(me, q, 2 * own).wait_send())
    for turn in range(max(iters - 2, 0), iters):
        grad_copy(turn % 2).wait_send()


def shards(
    tile_values,
    row_blocks,
    col_blocks,
    path_cost,
    path_bound,
    primal_start,
    dual_start,
    row_limits,
    step_size,
    weight_start,
    restart_flags,
):
    n = lax.axis_size("path")
    count = row_blocks.shape[2]
    half = path_cost.shape[0] // LANES
    own = dual_start.shape[0] // LANES
    vmem = pl.BlockSpec(memory_space=pltpu.VMEM)
    smem = pl.BlockSpec(memory_space=pltpu.SMEM)
    dma = pltpu.SemaphoreType.DMA
    primal, dual, loads = pl.pallas_call(
        functools.partial(kernel, n, restart_flags.shape[0]),
        out_shape=(
            jax.ShapeDtypeStruct((half, LANES), jnp.float32),
            jax.ShapeDtypeStruct((own, LANES), jnp.float32),
            jax.ShapeDtypeStruct((own, LANES), jnp.float32),
        ),
        in_specs=[
            pl.BlockSpec(memory_space=pl.ANY),
            smem,
            smem,
            vmem,
            vmem,
            vmem,
            vmem,
            vmem,
            smem,
            smem,
            smem,
        ],
        out_specs=(vmem, vmem, vmem),
        scratch_shapes=[
            pltpu.VMEM((count, LANES, LANES), jnp.bfloat16),
            pltpu.VMEM((count, LANES, LANES), jnp.bfloat16),
            pltpu.VMEM((2, 3, half, LANES), jnp.float32),
            pltpu.VMEM((2, 2 * half, LANES), jnp.float32),
            pltpu.VMEM((n, own + 2, LANES), jnp.float32),
            pltpu.VMEM((2, 2 * half + 8, LANES), jnp.float32),
            pltpu.VMEM((2, 2 * half + 8, LANES), jnp.float32),
            pltpu.VMEM((n, 2 * own, LANES), jnp.float32),
            pltpu.VMEM((n, 2 * own, LANES), jnp.float32),
            dma,
            dma,
            dma,
            dma((n,)),
            dma((n,)),
            dma((2,)),
            dma((2,)),
            dma((n,)),
            dma((n,)),
        ],
        compiler_params=pltpu.CompilerParams(
            collective_id=0, has_side_effects=True, vmem_limit_bytes=32 * 1024 * 1024
        ),
    )(
        tile_values,
        row_blocks.reshape(count),
        col_blocks.reshape(count),
        path_cost.reshape(half, LANES),
        path_bound.reshape(half, LANES),
        primal_start.reshape(half, LANES),
        dual_start.reshape(own, LANES),
        row_limits.reshape(own, LANES),
        step_size,
        weight_start,
        restart_flags,
    )
    return (primal.reshape(-1), dual.reshape(-1), loads.reshape(-1))


def solution(mesh):
    in_specs = (
        P(("groups", "path"), "cons", None, None, None),
        P(("groups", "path"), "cons", None),
        P(("groups", "path"), "cons", None),
        P(("groups", "path", "cons")),
        P(("groups", "path", "cons")),
        P(("groups", "path", "cons")),
        P(("groups", "path", "cons")),
        P(("groups", "path", "cons")),
        P("groups"),
        P("groups"),
        P("groups"),
    )
    out_specs = (
        P(("groups", "path", "cons")),
        P(("groups", "path", "cons")),
        P(("groups", "path", "cons")),
    )
    return jax.shard_map(shards, mesh=mesh, in_specs=in_specs, out_specs=out_specs, check_vma=False)
```

time: 358 us -> 65.7 us (0.18)
  blocking collectives: 193 us -> 0 us
  Pallas kernels: 0 us -> 59.9 us
  starting transfers between devices: 51.1 us -> 0 us
  waiting for transfers between devices: 47.8 us -> 0 us
  local copies, waits for them, and re-layouts: 29 us -> 3.64 us
  between operations: 14 us -> 2 us
  other arithmetic: 11.6 us -> 0 us
  matrix products: 10.6 us -> 0 us
    psum x5 -> x0, blocking collectives: 166 us -> none  [shards(): lax.psum((jnp.sum(primal_shift * primal_shift), jnp.sum(dual_shift * dual...]
    pallas_call x0 -> x1, Pallas kernels: none -> 59.9 us  [shards(): pl.pallas_call(functools.partial(kernel, n, restart_flags.shape[0]), out_...]
    all_to_all x14 -> x0, starting transfers between devices: 51.1 us -> none  [the longest x7 23.6 us: primal_product(): lax.all_to_all(outgoing, 'path', split_axis=0, concat_axis=0, tiled=True)]
    all_to_all x14 -> x0, waiting for transfers between devices: 47.8 us -> none  [the longest x7 38.7 us: primal_product(): lax.all_to_all(outgoing, 'path', split_axis=0, concat_axis=0, tiled=True)]
    gather x19 -> x0, local copies, waits for them, and re-layouts: 15 us -> none  [the longest x6 7.33 us: shards(): replies = dual_low.reshape(own_blocks, edge)[reply_rows]]
    unnamed x6 -> x0, blocking collectives: 14.8 us -> none
    all_gather x7 -> x0, blocking collectives: 12.4 us -> none  [primal_product(): primal_low = lax.all_gather(primal_low, 'cons', axis=0, tiled=True)]
    dot_general x20 -> x0, matrix products: 10.6 us -> none  [the longest x7 4.44 us: tile_rows(): jnp.einsum('tij,tj->ti', tile_values, picked, preferred_element_type=jnp....]
  transfers between devices with their start and end apart: 14 -> 0, of which waited for: 9 -> 0; matrix products, arithmetic and copies ran while one was open for 1% -> 0% of each run, Pallas kernels for 0% -> 0%
where the time goes in v1:
time: 65.7 us; the launch traced here: 65.5 us
  Pallas kernels  59.9 us (91%)
  local copies, waits for them, and re-layouts  3.64 us (6%)
  between operations  2 us (3%)
    pallas_call x1, Pallas kernels, shards(): pl.pallas_call(functools.partial(kernel, n, restart_flags.shape[0]), out_...  59.9 us
    unnamed x21, local copies, waits for them, and re-layouts  3.64 us

profile of v1, /device:TPU:0, one launch (start us, length us, event | category | flops | bytes accessed | tf_op | source)
XLA Modules:
  0.0 65.5 jit_solution(16113119546978512414)
XLA Ops:
  1.9 0.0 copy-start.8
  1.9 0.0 copy-start.5
  1.9 0.0 copy-start.7
  2.0 0.0 copy-start.3
  2.0 0.0 copy-start.2
  2.0 0.0 copy-start.1
  2.0 0.0 copy-start.4
  2.0 0.0 copy-start.6
  2.0 0.6 copy-done.8
  2.6 0.0 copy-done.5
  2.6 0.0 copy-done.7
  2.6 0.0 copy-done.3
  2.7 0.0 copy-done.2
  2.7 0.0 copy-done.1
  2.7 0.0 copy-done.4
  2.7 0.0 copy-done.6
  2.7 0.0 copy-start
  2.7 1.2 %copy-done = bf16[1,1,32,128,128]{4,3,2,1,0:T(8,128)(2,1)S(1)} copy-done((bf16[1,1,32,128,128]{4,3,2,1,0:T(8,128)(2,1)S(1)}, bf16[1,1,32,128,128]{4,3,2,1,0:T(8,128)(2,1)}, u32[]{:S(2)}) %copy-start) | copy-done | bytes 1048600
  3.9 59.9 %shard_map.130 = (f32[4,128]{1,0:T(4,128)S(1)}, f32[2,128]{1,0:T(2,128)S(1)}, f32[2,128]{1,0:T(2,128)S(1)}) custom-call(bf16[1,1,32,128,128]{4,3,2,1,0:T(8,128)(2,1)S(1)} %copy-done, s32[32]{0:T(128)S(1)} %bitcast.18, s32[32]{0:T(128)S(1)} %bitcast.19, f32[4,128]{1,0:T(4,128)S(1)} %bitcast.10, f32[4,128]{1,0:T(4,128)S(1)} %bitcast.11, ...), custom_call_target="tpu_custom_call" | custom-call | tf_op jit(solution)/shard_map/pallas_call | solution.py:246
  63.8 0.6 copy.19
  64.4 0.6 copy.20
  64.9 0.6 copy.21
Async XLA Ops:
  1.9 0.7 %copy-start.8 = (s32[6]{0:T(128)S(1)}, s32[6]{0:T(128)}, u32[]{:S(2)}) copy-start(s32[6]{0:T(128)} %flags_s.1) | copy-start | bytes 76
  1.9 0.7 %copy-start.5 = (f32[256]{0:T(256)S(1)}, f32[256]{0:T(256)}, u32[]{:S(2)}) copy-start(f32[256]{0:T(256)} %param.18) | copy-start | bytes 3076
  1.9 0.7 %copy-start.7 = (s32[1,1,32]{2,1,0:T(1,128)S(1)}, s32[1,1,32]{2,1,0:T(1,128)}, u32[]{:S(2)}) copy-start(s32[1,1,32]{2,1,0:T(1,128)} %param.13) | copy-start | bytes 388
  2.0 0.7 %copy-start.3 = (f32[512]{0:T(512)S(1)}, f32[512]{0:T(512)}, u32[]{:S(2)}) copy-start(f32[512]{0:T(512)} %param.16) | copy-start | bytes 6148
  2.0 0.7 %copy-start.2 = (f32[512]{0:T(512)S(1)}, f32[512]{0:T(512)}, u32[]{:S(2)}) copy-start(f32[512]{0:T(512)} %param.15) | copy-start | bytes 6148
  2.0 0.7 %copy-start.1 = (f32[512]{0:T(512)S(1)}, f32[512]{0:T(512)}, u32[]{:S(2)}) copy-start(f32[512]{0:T(512)} %param.14) | copy-start | bytes 6148
  2.0 0.7 %copy-start.4 = (f32[256]{0:T(256)S(1)}, f32[256]{0:T(256)}, u32[]{:S(2)}) copy-start(f32[256]{0:T(256)} %param.17) | copy-start | bytes 3076
  2.0 0.7 %copy-start.6 = (s32[1,1,32]{2,1,0:T(1,128)S(1)}, s32[1,1,32]{2,1,0:T(1,128)}, u32[]{:S(2)}) copy-start(s32[1,1,32]{2,1,0:T(1,128)} %param.12) | copy-start | bytes 388
  2.7 1.2 %copy-start = (bf16[1,1,32,128,128]{4,3,2,1,0:T(8,128)(2,1)S(1)}, bf16[1,1,32,128,128]{4,3,2,1,0:T(8,128)(2,1)}, u32[]{:S(2)}) copy-start(bf16[1,1,32,128,128]{4,3,2,1,0:T(8,128)(2,1)} %tiles_hbm.1) | copy-start | bytes 3145732

commit v2 on v1

--- a/solution.py
+++ b/solution.py
@@ -32,8 +32,11 @@
     start_buf,
     flows,
     dual_buf,
+    dual_all,
+    limit_all,
     grad_out,
     grad_in,
+    act_all,
     act_out,
     act_in,
     tile_sem,
@@ -43,6 +46,8 @@
     dual_recv,
     grad_send,
     grad_recv,
+    all_send,
+    all_recv,
     act_send,
     act_recv,
 ):
@@ -72,7 +77,7 @@
     start_buf[core, 1] = bound_in[...]
     start_buf[core, 2] = primal_in[...]
     dual_buf[me, pl.ds(0, own)] = dual_in[...]
-    dual_buf[me, pl.ds(own, 2)] = jnp.zeros((2, LANES), jnp.float32)
+    dual_buf[me, pl.ds(own, own)] = limits_in[...]
     pl.semaphore_wait(barrier, n)
 
     def dual_copy(source, q):
@@ -84,10 +89,19 @@
             device_id={"path": q},
         )
 
-    def act_copy(source, q, rows):
-        return pltpu.make_async_remote_copy(
-            src_ref=act_out.at[q, pl.ds(0, rows)],
-            dst_ref=act_in.at[source, pl.ds(0, rows)],
+    def all_copy(slot, source, q):
+        return pltpu.make_async_remote_copy(
+            src_ref=act_all.at[slot, source],
+            dst_ref=act_all.at[slot, source],
+            send_sem=all_send.at[slot, q],
+            recv_sem=all_recv.at[slot, source],
+            device_id={"path": q},
+        )
+
+    def act_copy(source, q):
+        return pltpu.make_async_remote_copy(
+            src_ref=act_out.at[q],
+            dst_ref=act_in.at[source],
             send_sem=act_send.at[q],
             recv_sem=act_recv.at[source],
             device_id={"path": q},
@@ -123,8 +137,15 @@
 
     cost, bound, primal = whole(0), whole(1), whole(2)
     start_copy(core).wait_send()
-    dual = dual_in[...]
-    limits = limits_in[...]
+    peers(lambda q: dual_copy(q, q).wait_recv())
+    for q in range(n):
+        dual_all[pl.ds(q * own, own)] = dual_buf[q, pl.ds(0, own)]
+        limit_all[pl.ds(q * own, own)] = dual_buf[q, pl.ds(own, own)]
+    dual = dual_all[...]
+    limits = limit_all[...]
+    peers(lambda q: dual_copy(me, q).wait_send())
+    moves = jnp.zeros((1, LANES), jnp.float32)
+    primal_moves = moves
     eta = step_s[0]
     weight = jnp.full((1, LANES), weight_s[0], jnp.float32)
     anchor_primal, anchor_dual = primal, dual
@@ -135,11 +156,9 @@
     for turn in range(iters):
         slot = turn % 2
         last = turn == iters - 1
-        peers(lambda q: dual_copy(q, q).wait_recv())
         parts = []
         for t in range(count):
-            row = rows_s[t]
-            line = dual_buf[row // own, pl.ds(row % own, 1)]
+            line = dual_all[pl.ds(rows_s[t], 1)]
             parts.append(jnp.where(col_iota == cols_s[t], line, 0.0).astype(jnp.bfloat16))
         left = jnp.concatenate(parts, axis=1)
         partial = jnp.dot(
@@ -148,10 +167,8 @@
         if turn >= 2:
             grad_copy(slot).wait_send()
         grad_out[slot, pl.ds(0, blocks)] = partial
-        moves = jnp.sum(dual_buf[:, own, :], axis=0, keepdims=True)
         grad_out[slot, pl.ds(blocks, 8)] = jnp.broadcast_to(moves, (8, LANES))
         grad_copy(slot).start()
-        primal_moves = jnp.sum(dual_buf[:, own + 1, :], axis=0, keepdims=True)
         primal_move = jnp.sum(primal_moves, axis=1, keepdims=True)
         grad_copy(slot).wait_recv()
         gradient = partial + grad_in[slot, pl.ds(0, blocks)]
@@ -178,8 +195,6 @@
         row_iota = lax.broadcasted_iota(jnp.int32, (n * rows, LANES), 0)
         parts = []
         lines = [extrapolated, primal] if last else [extrapolated]
-        if turn > 0:
-            peers(lambda q: act_copy(me, q, own).wait_send())
         for index, line in enumerate(lines):
             flows[index] = line
         for t in range(count):
@@ -194,31 +209,45 @@
         activity = jnp.dot(
             left, turned[...].reshape(count * LANES, LANES), preferred_element_type=jnp.float32
         )
-        for q in range(n):
-            act_out[q, pl.ds(0, rows)] = activity[q * rows : (q + 1) * rows]
-        peers(lambda q: act_copy(me, q, rows).start())
-        act_in[me, pl.ds(0, rows)] = act_out[me, pl.ds(0, rows)]
-        peers(lambda q: dual_copy(me, q).wait_send())
-        peers(lambda q: act_copy(q, q, rows).wait_recv())
-        total = jnp.sum(act_in[:, pl.ds(0, rows)], axis=0)
-        dual_next = jnp.maximum(dual + eta * weight * (total[:own] - limits), 0.0)
-        dual_sum = dual_sum + dual_next
-        dual_mean = dual_sum / taken
-        shift = dual_mean - anchor_dual
-        dual = jnp.where(restart, dual_mean, dual_next)
-        anchor_dual = jnp.where(restart, dual_mean, anchor_dual)
-        dual_sum = jnp.where(restart, 0.0, dual_sum)
-        taken = jnp.where(restart, 0.0, taken)
-        if not last:
-            dual_buf[me, pl.ds(0, own)] = dual
-            dual_buf[me, pl.ds(own, 1)] = jnp.sum(shift * shift, axis=0, keepdims=True)
-            dual_buf[me, pl.ds(own + 1, 1)] = primal_part
-            peers(lambda q: dual_copy(me, q).start())
+        if last:
+            for q in range(n):
+                act_out[q] = activity[q * rows : (q + 1) * rows]
+            peers(lambda q: act_copy(me, q).start())
+            act_in[me] = act_out[me]
+            mine = pl.ds(me * own, own)
+            dual = dual_all[mine]
+            limit_all[...] = dual_sum
+            dual_sum = limit_all[mine]
+            peers(lambda q: act_copy(q, q).wait_recv())
+            total = jnp.sum(act_in[...], axis=0)
+            dual_next = jnp.maximum(dual + eta * weight * (total[:own] - limits_in[...]), 0.0)
+            dual = jnp.where(restart, (dual_sum + dual_next) / taken, dual_next)
+        else:
+            if turn >= 2:
+                peers(lambda q: all_copy(slot, me, q).wait_send())
+            act_all[slot, me, pl.ds(0, n * own)] = activity
+            act_all[slot, me, pl.ds(n * own, 1)] = primal_part
+            peers(lambda q: all_copy(slot, me, q).start())
+            peers(lambda q: all_copy(slot, q, q).wait_recv())
+            total = jnp.sum(act_all[slot, :, pl.ds(0, n * own)], axis=0)
+            primal_moves = jnp.sum(act_all[slot, :, n * own, :], axis=0, keepdims=True)
+            dual_next = jnp.maximum(dual + eta * weight * (total - limits), 0.0)
+            dual_sum = dual_sum + dual_next
+            dual_mean = dual_sum / taken
+            shift = dual_mean - anchor_dual
+            moves = jnp.sum(shift * shift, axis=0, keepdims=True)
+            dual = jnp.where(restart, dual_mean, dual_next)
+            anchor_dual = jnp.where(restart, dual_mean, anchor_dual)
+            dual_sum = jnp.where(restart, 0.0, dual_sum)
+            taken = jnp.where(restart, 0.0, taken)
+            dual_all[...] = dual
 
     primal_out[...] = jnp.where(core == 0, primal[:half], primal[half:])
     dual_out[...] = dual
     loads_out[...] = total[own:]
-    peers(lambda q: act_copy(me, q, 2 * own).wait_send())
+    peers(lambda q: act_copy(me, q).wait_send())
+    for turn in range(max(iters - 3, 0), iters - 1):
+        peers(functools.partial(lambda slot, q: all_copy(slot, me, q).wait_send(), turn % 2))
     for turn in range(max(iters - 2, 0), iters):
         grad_copy(turn % 2).wait_send()
 
@@ -269,9 +298,12 @@
             pltpu.VMEM((count, LANES, LANES), jnp.bfloat16),
             pltpu.VMEM((2, 3, half, LANES), jnp.float32),
             pltpu.VMEM((2, 2 * half, LANES), jnp.float32),
-            pltpu.VMEM((n, own + 2, LANES), jnp.float32),
+            pltpu.VMEM((n, 2 * own, LANES), jnp.float32),
+            pltpu.VMEM((n * own, LANES), jnp.float32),
+            pltpu.VMEM((n * own, LANES), jnp.float32),
             pltpu.VMEM((2, 2 * half + 8, LANES), jnp.float32),
             pltpu.VMEM((2, 2 * half + 8, LANES), jnp.float32),
+            pltpu.VMEM((2, n, n * own + 1, LANES), jnp.float32),
             pltpu.VMEM((n, 2 * own, LANES), jnp.float32),
             pltpu.VMEM((n, 2 * own, LANES), jnp.float32),
             dma,
@@ -281,6 +313,8 @@
             dma((n,)),
             dma((2,)),
             dma((2,)),
+            dma((2, n)),
+            dma((2, n)),
             dma((n,)),
             dma((n,)),
         ],

time: 65.7 us -> 49.5 us (0.75)
  Pallas kernels: 59.9 us -> 43.7 us
    pallas_call x1, Pallas kernels: 59.9 us -> 43.7 us  [shards(): pl.pallas_call(functools.partial(kernel, n, restart_flags.shape[0]), out_...]
where the time goes in v2:
time: 49.5 us; the launch traced here: 49.3 us
  Pallas kernels  43.7 us (88%)
  local copies, waits for them, and re-layouts  3.64 us (7%)
  between operations  2 us (4%)
    pallas_call x1, Pallas kernels, shards(): pl.pallas_call(functools.partial(kernel, n, restart_flags.shape[0]), out_...  43.7 us
    unnamed x21, local copies, waits for them, and re-layouts  3.64 us

profile of v2, /device:TPU:0, one launch (start us, length us, event | category | flops | bytes accessed | tf_op | source)
XLA Modules:
  0.0 49.3 jit_solution(16813345831013811783)
XLA Ops:
  1.9 0.0 copy-start.8
  1.9 0.0 copy-start.5
  1.9 0.0 copy-start.7
  2.0 0.0 copy-start.3
  2.0 0.0 copy-start.2
  2.0 0.0 copy-start.1
  2.0 0.0 copy-start.4
  2.0 0.0 copy-start.6
  2.0 0.6 %copy-done.8 = s32[6]{0:T(128)S(1)} copy-done((s32[6]{0:T(128)S(1)}, s32[6]{0:T(128)}, u32[]{:S(2)}) %copy-start.8) | copy-done | bytes 48
  2.6 0.0 copy-done.5
  2.6 0.0 copy-done.7
  2.6 0.0 copy-done.3
  2.7 0.0 copy-done.2
  2.7 0.0 copy-done.1
  2.7 0.0 copy-done.4
  2.7 0.0 copy-done.6
  2.7 0.0 copy-start
  2.7 1.2 %copy-done = bf16[1,1,32,128,128]{4,3,2,1,0:T(8,128)(2,1)S(1)} copy-done((bf16[1,1,32,128,128]{4,3,2,1,0:T(8,128)(2,1)S(1)}, bf16[1,1,32,128,128]{4,3,2,1,0:T(8,128)(2,1)}, u32[]{:S(2)}) %copy-start) | copy-done | bytes 1048600
  3.9 43.7 %shard_map.130 = (f32[4,128]{1,0:T(4,128)S(1)}, f32[2,128]{1,0:T(2,128)S(1)}, f32[2,128]{1,0:T(2,128)S(1)}) custom-call(bf16[1,1,32,128,128]{4,3,2,1,0:T(8,128)(2,1)S(1)} %copy-done, s32[32]{0:T(128)S(1)} %bitcast.18, s32[32]{0:T(128)S(1)} %bitcast.19, f32[4,128]{1,0:T(4,128)S(1)} %bitcast.10, f32[4,128]{1,0:T(4,128)S(1)} %bitcast.11, ...), custom_call_target="tpu_custom_call" | custom-call | tf_op jit(solution)/shard_map/pallas_call | solution.py:275
  47.6 0.6 %copy.19 = f32[512]{0:T(512)} copy(f32[512]{0:T(512)S(1)} %bitcast.13) | data formatting | bytes 4096
  48.2 0.6 %copy.20 = f32[256]{0:T(256)} copy(f32[256]{0:T(256)S(1)} %bitcast.15) | data formatting | bytes 2048
  48.7 0.6 %copy.21 = f32[256]{0:T(256)} copy(f32[256]{0:T(256)S(1)} %bitcast.14) | data formatting | bytes 2048
Async XLA Ops:
  1.9 0.7 %copy-start.8 = (s32[6]{0:T(128)S(1)}, s32[6]{0:T(128)}, u32[]{:S(2)}) copy-start(s32[6]{0:T(128)} %flags_s.1) | copy-start | bytes 76
  1.9 0.7 %copy-start.5 = (f32[256]{0:T(256)S(1)}, f32[256]{0:T(256)}, u32[]{:S(2)}) copy-start(f32[256]{0:T(256)} %param.18) | copy-start | bytes 3076
  1.9 0.7 %copy-start.7 = (s32[1,1,32]{2,1,0:T(1,128)S(1)}, s32[1,1,32]{2,1,0:T(1,128)}, u32[]{:S(2)}) copy-start(s32[1,1,32]{2,1,0:T(1,128)} %param.13) | copy-start | bytes 388
  2.0 0.7 %copy-start.3 = (f32[512]{0:T(512)S(1)}, f32[512]{0:T(512)}, u32[]{:S(2)}) copy-start(f32[512]{0:T(512)} %param.16) | copy-start | bytes 6148
  2.0 0.7 %copy-start.2 = (f32[512]{0:T(512)S(1)}, f32[512]{0:T(512)}, u32[]{:S(2)}) copy-start(f32[512]{0:T(512)} %param.15) | copy-start | bytes 6148
  2.0 0.7 %copy-start.1 = (f32[512]{0:T(512)S(1)}, f32[512]{0:T(512)}, u32[]{:S(2)}) copy-start(f32[512]{0:T(512)} %param.14) | copy-start | bytes 6148
  2.0 0.7 %copy-start.4 = (f32[256]{0:T(256)S(1)}, f32[256]{0:T(256)}, u32[]{:S(2)}) copy-start(f32[256]{0:T(256)} %param.17) | copy-start | bytes 3076
  2.0 0.7 %copy-start.6 = (s32[1,1,32]{2,1,0:T(1,128)S(1)}, s32[1,1,32]{2,1,0:T(1,128)}, u32[]{:S(2)}) copy-start(s32[1,1,32]{2,1,0:T(1,128)} %param.12) | copy-start | bytes 388
  2.7 1.2 %copy-start = (bf16[1,1,32,128,128]{4,3,2,1,0:T(8,128)(2,1)S(1)}, bf16[1,1,32,128,128]{4,3,2,1,0:T(8,128)(2,1)}, u32[]{:S(2)}) copy-start(bf16[1,1,32,128,128]{4,3,2,1,0:T(8,128)(2,1)} %tiles_hbm.1) | copy-start | bytes 3145732

commit v3 on v2

--- a/solution.py
+++ b/solution.py
@@ -40,6 +40,7 @@
     act_out,
     act_in,
     tile_sem,
+    fetch_sem,
     start_send,
     start_recv,
     dual_send,
@@ -60,24 +61,41 @@
     blocks = 2 * half
     unroll = n <= 8
 
+    flips = []
+    if n == 8:
+        bits = [lax.rem(me // (1 << i), 2) for i in range(3)]
+        for k in range(7, 0, -1):
+            flips.append(me + sum((1 << i) * (1 - 2 * bits[i]) for i in range(3) if k >> i & 1))
+
     def peers(body):
         def step(k, carry):
             body(lax.rem(me + k, n))
             return carry
 
+        if flips:
+            for q in flips:
+                body(q)
+            return
+
         lax.fori_loop(1, n, step, 0, unroll=unroll)
 
     tile_copy = pltpu.make_async_copy(tiles_hbm.at[0, 0], tiles, tile_sem)
+    fetches = [
+        pltpu.make_async_copy(dual_in, dual_buf.at[me, pl.ds(0, own)], fetch_sem.at[0]),
+        pltpu.make_async_copy(limits_in, dual_buf.at[me, pl.ds(own, own)], fetch_sem.at[1]),
+        pltpu.make_async_copy(cost_in, start_buf.at[core, 0], fetch_sem.at[2]),
+        pltpu.make_async_copy(bound_in, start_buf.at[core, 1], fetch_sem.at[3]),
+        pltpu.make_async_copy(primal_in, start_buf.at[core, 2], fetch_sem.at[4]),
+    ]
+    for copy in fetches:
+        copy.start()
     tile_copy.start()
     barrier = pltpu.get_barrier_semaphore()
     peers(lambda q: pl.semaphore_signal(barrier, inc=1, device_id={"path": q}))
     pl.semaphore_signal(barrier, inc=1, device_id={"cons": other})
 
-    start_buf[core, 0] = cost_in[...]
-    start_buf[core, 1] = bound_in[...]
-    start_buf[core, 2] = primal_in[...]
-    dual_buf[me, pl.ds(0, own)] = dual_in[...]
-    dual_buf[me, pl.ds(own, own)] = limits_in[...]
+    for copy in fetches:
+        copy.wait()
     pl.semaphore_wait(barrier, n)
 
     def dual_copy(source, q):
@@ -156,6 +174,12 @@
     for turn in range(iters):
         slot = turn % 2
         last = turn == iters - 1
+        if turn >= 2:
+            grad_copy(slot).wait_send()
+        dual_move = jnp.sum(moves, axis=1, keepdims=True)
+        grad_out[slot, pl.ds(blocks, 8)] = jnp.broadcast_to(dual_move, (8, LANES))
+        primal_move = jnp.sum(primal_moves, axis=1, keepdims=True)
+        primal_root = jnp.sqrt(primal_move + EPSILON)
         parts = []
         for t in range(count):
             line = dual_all[pl.ds(rows_s[t], 1)]
@@ -164,20 +188,13 @@
         partial = jnp.dot(
             left, tiles[...].reshape(count * LANES, LANES), preferred_element_type=jnp.float32
         )
-        if turn >= 2:
-            grad_copy(slot).wait_send()
         grad_out[slot, pl.ds(0, blocks)] = partial
-        grad_out[slot, pl.ds(blocks, 8)] = jnp.broadcast_to(moves, (8, LANES))
         grad_copy(slot).start()
-        primal_move = jnp.sum(primal_moves, axis=1, keepdims=True)
         grad_copy(slot).wait_recv()
         gradient = partial + grad_in[slot, pl.ds(0, blocks)]
         if turn > 0:
-            moves = moves + grad_in[slot, pl.ds(blocks, 1)]
-            dual_move = jnp.sum(moves, axis=1, keepdims=True)
-            candidate = jnp.sqrt(
-                weight * jnp.sqrt(dual_move + EPSILON) / jnp.sqrt(primal_move + EPSILON)
-            )
+            dual_move = dual_move + grad_in[slot, pl.ds(blocks, 1)]
+            candidate = jnp.sqrt(weight * jnp.sqrt(dual_move + EPSILON) / primal_root)
             weight = jnp.where(flags_s[turn - 1] == 1, candidate, weight)
         restart = flags_s[turn] == 1
         primal_next = jnp.clip(primal - eta / weight * (cost + gradient), 0.0, bound)
@@ -220,7 +237,7 @@
             dual_sum = limit_all[mine]
             peers(lambda q: act_copy(q, q).wait_recv())
             total = jnp.sum(act_in[...], axis=0)
-            dual_next = jnp.maximum(dual + eta * weight * (total[:own] - limits_in[...]), 0.0)
+            dual_next = jnp.maximum(dual + eta * weight * (total[:own] - dual_buf[me, pl.ds(own, own)]), 0.0)
             dual = jnp.where(restart, (dual_sum + dual_next) / taken, dual_next)
         else:
             if turn >= 2:
@@ -271,6 +288,7 @@
     own = dual_start.shape[0] // LANES
     vmem = pl.BlockSpec(memory_space=pltpu.VMEM)
     smem = pl.BlockSpec(memory_space=pltpu.SMEM)
+    hbm = pl.BlockSpec(memory_space=pltpu.HBM)
     dma = pltpu.SemaphoreType.DMA
     primal, dual, loads = pl.pallas_call(
         functools.partial(kernel, n, restart_flags.shape[0]),
@@ -280,14 +298,14 @@
             jax.ShapeDtypeStruct((own, LANES), jnp.float32),
         ),
         in_specs=[
-            pl.BlockSpec(memory_space=pl.ANY),
-            smem,
-            smem,
-            vmem,
-            vmem,
-            vmem,
-            vmem,
-            vmem,
+            hbm,
+            smem,
+            smem,
+            hbm,
+            hbm,
+            hbm,
+            hbm,
+            hbm,
             smem,
             smem,
             smem,
@@ -307,6 +325,7 @@
             pltpu.VMEM((n, 2 * own, LANES), jnp.float32),
             pltpu.VMEM((n, 2 * own, LANES), jnp.float32),
             dma,
+            dma((5,)),
             dma,
             dma,
             dma((n,)),
@@ -319,7 +338,7 @@
             dma((n,)),
         ],
         compiler_params=pltpu.CompilerParams(
-            collective_id=0, has_side_effects=True, vmem_limit_bytes=32 * 1024 * 1024
+            collective_id=0, has_side_effects=True, vmem_limit_bytes=63 * 1024 * 1024
         ),
     )(
         tile_values,

time: 49.5 us -> 47.4 us (0.958)
  local copies, waits for them, and re-layouts: 3.64 us -> 2.51 us
  Pallas kernels: 43.7 us -> 42.7 us
    unnamed x21 -> x9, local copies, waits for them, and re-layouts: 3.64 us -> 2.51 us
    pallas_call x1, Pallas kernels: 43.7 us -> 42.7 us  [shards(): pl.pallas_call(functools.partial(kernel, n, restart_flags.shape[0]), out_...]
where the time goes in v3:
time: 47.4 us; the launch traced here: 47.2 us
  Pallas kernels  42.7 us (90%)
  local copies, waits for them, and re-layouts  2.51 us (5%)
  between operations  1.94 us (4%)
    pallas_call x1, Pallas kernels, shards(): pl.pallas_call(functools.partial(kernel, n, restart_flags.shape[0]), out_...  42.7 us
    unnamed x9, local copies, waits for them, and re-layouts  2.51 us

profile of v3, /device:TPU:0, one launch (start us, length us, event | category | flops | bytes accessed | tf_op | source)
XLA Modules:
  0.0 47.2 jit_solution(2912172331415829774)
XLA Ops:
  1.9 42.7 %shard_map.130 = (f32[4,128]{1,0:T(4,128)}, f32[2,128]{1,0:T(2,128)}, f32[2,128]{1,0:T(2,128)}) custom-call(bf16[1,1,32,128,128]{4,3,2,1,0:T(8,128)(2,1)} %tiles_hbm.1, s32[32]{0:T(128)} %bitcast.18, s32[32]{0:T(128)} %bitcast.19, f32[4,128]{1,0:T(4,128)} %bitcast.10, f32[4,128]{1,0:T(4,128)} %bitcast.11, f32[4,128]{1,0:T(4,128)} %bitcast.12, ...), custom_call_target="tpu_custom_call" | custom-call | tf_op jit(solution)/shard_map/pallas_call | solution.py:293
  44.7 0.0 copy-start
  44.7 0.6 %copy-done = f32[4,128]{1,0:T(4,128)S(1)} copy-done((f32[4,128]{1,0:T(4,128)S(1)}, f32[4,128]{1,0:T(4,128)}, u32[]{:S(2)}) %copy-start) | copy-done | bytes 2072
  45.3 0.0 copy-start.2
  45.3 0.6 %copy.19 = f32[512]{0:T(512)} copy(f32[512]{0:T(512)S(1)} %bitcast.13) | data formatting | bytes 4096
  45.9 0.1 copy-done.2
  46.0 0.0 copy-start.1
  46.0 0.6 %copy.20 = f32[256]{0:T(256)} copy(f32[256]{0:T(256)S(1)} %bitcast.15) | data formatting | bytes 2048
  46.5 0.1 copy-done.1
  46.6 0.6 %copy.21 = f32[256]{0:T(256)} copy(f32[256]{0:T(256)S(1)} %bitcast.14) | data formatting | bytes 2048
Async XLA Ops:
  44.7 0.7 %copy-start = (f32[4,128]{1,0:T(4,128)S(1)}, f32[4,128]{1,0:T(4,128)}, u32[]{:S(2)}) copy-start(f32[4,128]{1,0:T(4,128)} %get-tuple-element.6) | copy-start | bytes 6148
  45.3 0.6 %copy-start.2 = (f32[2,128]{1,0:T(2,128)S(1)}, f32[2,128]{1,0:T(2,128)}, u32[]{:S(2)}) copy-start(f32[2,128]{1,0:T(2,128)} %get-tuple-element.7) | copy-start | bytes 3076
  46.0 0.7 %copy-start.1 = (f32[2,128]{1,0:T(2,128)S(1)}, f32[2,128]{1,0:T(2,128)}, u32[]{:S(2)}) copy-start(f32[2,128]{1,0:T(2,128)} %get-tuple-element.8) | copy-start | bytes 3076

commit v4 on v3

--- a/solution.py
+++ b/solution.py
@@ -24,9 +24,7 @@
     step_s,
     weight_s,
     flags_s,
-    primal_out,
-    dual_out,
-    loads_out,
+    result,
     tiles,
     turned,
     start_buf,
@@ -259,9 +257,9 @@
             taken = jnp.where(restart, 0.0, taken)
             dual_all[...] = dual
 
-    primal_out[...] = jnp.where(core == 0, primal[:half], primal[half:])
-    dual_out[...] = dual
-    loads_out[...] = total[own:]
+    result[pl.ds(0, half)] = jnp.where(core == 0, primal[:half], primal[half:])
+    result[pl.ds(half, own)] = dual
+    result[pl.ds(half + own, own)] = total[own:]
     peers(lambda q: act_copy(me, q).wait_send())
     for turn in range(max(iters - 3, 0), iters - 1):
         peers(functools.partial(lambda slot, q: all_copy(slot, me, q).wait_send(), turn % 2))
@@ -290,13 +288,9 @@
     smem = pl.BlockSpec(memory_space=pltpu.SMEM)
     hbm = pl.BlockSpec(memory_space=pltpu.HBM)
     dma = pltpu.SemaphoreType.DMA
-    primal, dual, loads = pl.pallas_call(
+    result = pl.pallas_call(
         functools.partial(kernel, n, restart_flags.shape[0]),
-        out_shape=(
-            jax.ShapeDtypeStruct((half, LANES), jnp.float32),
-            jax.ShapeDtypeStruct((own, LANES), jnp.float32),
-            jax.ShapeDtypeStruct((own, LANES), jnp.float32),
-        ),
+        out_shape=jax.ShapeDtypeStruct((half + 2 * own, LANES), jnp.float32),
         in_specs=[
             hbm,
             smem,
@@ -310,7 +304,7 @@
             smem,
             smem,
         ],
-        out_specs=(vmem, vmem, vmem),
+        out_specs=vmem,
         scratch_shapes=[
             pltpu.VMEM((count, LANES, LANES), jnp.bfloat16),
             pltpu.VMEM((count, LANES, LANES), jnp.bfloat16),
@@ -353,7 +347,9 @@
         weight_start,
         restart_flags,
     )
-    return (primal.reshape(-1), dual.reshape(-1), loads.reshape(-1))
+    flat = result.reshape(-1)
+    first, second = half * LANES, (half + own) * LANES
+    return (flat[:first], flat[first:second], flat[second:])
 
 
 def solution(mesh):

time: 47.4 us -> 46.8 us (0.987)
  local copies, waits for them, and re-layouts: 2.51 us -> 1.92 us
    unnamed x9 -> x2, local copies, waits for them, and re-layouts: 2.51 us -> 0.01 us
    slice x0 -> x2, local copies, waits for them, and re-layouts: none -> 1.92 us  [shards(): return (flat[:first], flat[first:second], flat[second:])]
where the time goes in v4:
time: 46.8 us; the launch traced here: 46.6 us
  Pallas kernels  42.7 us (91%)
  between operations  1.94 us (4%)
  local copies, waits for them, and re-layouts  1.92 us (4%)
    pallas_call x1, Pallas kernels, shards(): pl.pallas_call(functools.partial(kernel, n, restart_flags.shape[0]), out_...  42.7 us
    slice x2, local copies, waits for them, and re-layouts, shards(): return (flat[:first], flat[first:second], flat[second:])  1.92 us

profile of v4, /device:TPU:0, one launch (start us, length us, event | category | flops | bytes accessed | tf_op | source)
XLA Modules:
  0.0 46.6 jit_solution(1456495748056307862)
XLA Ops:
  1.9 42.7 %shard_map.130 = f32[8,128]{1,0:T(8,128)} custom-call(bf16[1,1,32,128,128]{4,3,2,1,0:T(8,128)(2,1)} %tiles_hbm.1, s32[32]{0:T(128)} %bitcast.18, s32[32]{0:T(128)} %bitcast.19, f32[4,128]{1,0:T(4,128)} %bitcast.13, f32[4,128]{1,0:T(4,128)} %bitcast.14, f32[4,128]{1,0:T(4,128)} %bitcast.15, f32[2,128]{1,0:T(2,128)} %bitcast.16, f32[2,128]{1,0:T(2,128)} %bitcast.17, ...), custom_call_target="tpu_custom_call" | custom-call | tf_op jit(solution)/shard_map/pallas_call | solution.py:291
  44.7 0.0 copy-start
  44.7 1.3 %slice_bitcast_fusion.1 = (f32[256]{0:T(256)}, f32[256]{0:T(256)}) fusion(f32[8,128]{1,0:T(8,128)} %shard_map.130), kind=kLoop, calls=%fused_computation.1 | loop fusion | bytes 4096 | tf_op jit(solution)/shard_map/slice | solution.py:352
  46.0 0.0 copy-done
  46.0 0.6 %slice_bitcast_fusion = f32[512]{0:T(512)} fusion(f32[8,128]{1,0:T(8,128)S(1)} %copy-done), kind=kLoop, calls=%fused_computation | loop fusion | bytes 4096 | tf_op jit(solution)/shard_map/slice | solution.py:352
Async XLA Ops:
  44.7 1.4 %copy-start = (f32[8,128]{1,0:T(8,128)S(1)}, f32[8,128]{1,0:T(8,128)}, u32[]{:S(2)}) copy-start(f32[8,128]{1,0:T(8,128)} %shard_map.130) | copy-start | bytes 12292
